TPU v7x, 32 devices: a whole 2x2x4 slice. The times are simulated.
32 devices in a mesh: blocks: 2 (over y), space: 4 (over z), tm: 2 (over x), span: 2 (over core).
Axes of the slice: x: 2, y: 2, z: 4, core: 2. Of those that a mesh axis runs over, the one named last changes fastest.
Arguments:
- snapshots: float32 [320, 64, 512], P(('blocks', 'tm'), 'space', 'span'), parts along dimension 0, may hold values from -6 to 6
- lagrange_weights: float32 [512, 6], P(('blocks', 'tm')), parts along dimension 0, may hold values from -3 to 3
- source_start: int32 [512], P(('blocks', 'tm')), parts along dimension 0, may hold values from 0 to 156
- band_len: int32 [512], P(('blocks', 'tm')), parts along dimension 0, may hold values from 4 to 6
- band_list: int32 [8], replicated, may hold values from 0 to 15, as said below
- row_metric: float32 [64], P('space'), may hold values from 0.5 to 2
Outputs:
- spectra: float32 [256, 2, 64, 512], P(('blocks', 'space', 'tm'), None, None, 'span'), parts along dimension 0
There are 2 independent parts, one for each index of `blocks`. A program takes and returns all parts, laid end to end along the dimension named above; an argument that names none is the same for every part. Nothing has to cross between parts.
Inputs may be any that keep to these rules, and one draw needn't show every extreme that they name: `band_list`: 8 distinct band numbers.
All inputs are finite; a program needn't handle non-finite values.
Results may differ from a plain program's by a relative error of at most 0.0001.
Values sent between devices are 32-bit elements; how exact they have to be, the bound alone decides.
A program may use at most 64 MiB of HBM per device.

v0:
```python
import math
import jax
import jax.numpy as jnp
from jax import lax
from jax.sharding import PartitionSpec as P

HALO = 16
NT = 256
BW = 8
NL = 8


def extended(cells, sides, width, closed):
    for axis, dim in sides:
        count = lax.axis_size(axis)
        ends = count if closed else count - 1
        head = lax.slice_in_dim(cells, 0, width, axis=dim)
        tail = lax.slice_in_dim(cells, cells.shape[dim] - width, cells.shape[dim], axis=dim)
        cells = jnp.concatenate(
            [
                lax.ppermute(tail, axis, [(i, (i + 1) % count) for i in range(ends)]),
                cells,
                lax.ppermute(head, axis, [((i + 1) % count, i) for i in range(ends)]),
            ],
            axis=dim,
        )
    return cells


def dft_rows(band_list, row_ids, first_sample, count):
    listed_idx = row_ids // 2
    is_imag = row_ids % 2
    band_pos = listed_idx // BW
    matches = band_pos[:, None] == jnp.arange(band_list.shape[0])[None, :]
    band_of = jnp.sum(jnp.where(matches, band_list[None, :], 0), axis=1)
    frequency = band_of * BW + listed_idx % BW
    sample_ids = first_sample + jnp.arange(count)
    phase_idx = frequency[:, None] * sample_ids[None, :] % NT
    angles = 2.0 * math.pi / NT * phase_idx.astype(jnp.float32)
    window = 0.5 - 0.5 * jnp.cos(2.0 * math.pi / NT * sample_ids.astype(jnp.float32))
    weighting = window / math.sqrt(NT)
    waves = jnp.where(is_imag[:, None] == 0, jnp.cos(angles), -jnp.sin(angles))
    return waves * weighting[None, :]


def shards(snapshots, lagrange_weights, source_start, band_len, band_list, row_metric):
    tm_index = lax.axis_index("tm")
    n_tm, n_space = (lax.axis_size("tm"), lax.axis_size("space"))
    steps_dev, rows_dev, span_cells = snapshots.shape
    samples = source_start.shape[0]
    reach = extended(snapshots, (("tm", 0),), HALO, False)
    reach_len = steps_dev + 2 * HALO
    anchor = tm_index * steps_dev - HALO
    slot_ids = jnp.arange(6)
    columns = source_start[:, None] + slot_ids[None, :] - anchor
    active = slot_ids[None, :] < band_len[:, None]
    selected = (columns[:, :, None] == jnp.arange(reach_len)[None, None, :]) & active[:, :, None]
    interp_matrix = jnp.sum(
        jnp.where(selected, lagrange_weights[:, :, None], jnp.float32(0.0)), axis=1
    )
    total_rows = 2 * NL * BW
    own = total_rows // (n_tm * n_space)
    positions = jnp.arange(total_rows).reshape(n_space, n_tm, own).transpose(1, 0, 2).reshape(-1)
    coeffs = dft_rows(band_list, positions, tm_index * samples, samples)
    combined = jnp.dot(coeffs, interp_matrix, precision=lax.Precision.HIGHEST)
    partial = jnp.dot(
        combined, reach.reshape(reach_len, rows_dev * span_cells), precision=lax.Precision.HIGHEST
    )
    summed = lax.psum_scatter(partial, "tm", scatter_dimension=0, tiled=True)
    summed = summed.reshape(n_space * own, rows_dev, span_cells)
    fields = lax.all_to_all(summed, "space", split_axis=0, concat_axis=1, tiled=True)
    metric = lax.all_gather(row_metric, "space", tiled=True)
    row_padded = jnp.pad(fields, ((0, 0), (1, 1), (0, 0)))
    along_rows = 0.5 * metric[None, :, None] * (row_padded[:, 2:, :] - row_padded[:, :-2, :])
    span_padded = extended(fields, (("span", 2),), 1, True)
    along_span = 0.5 * (span_padded[:, :, 2:] - span_padded[:, :, :-2])
    return jnp.stack((along_rows, along_span), axis=1)


def solution(mesh):
    placed = (
        P(("blocks", "tm"), "space", "span"),
        P(("blocks", "tm"), None),
        P(("blocks", "tm")),
        P(("blocks", "tm")),
        P(),
        P("space"),
    )
    return jax.shard_map(
        shards,
        mesh=mesh,
        in_specs=placed,
        out_specs=P(("blocks", "space", "tm"), None, None, "span"),
        check_vma=False,
    )
```

profile of v0, /device:TPU:0, one launch (start us, length us, event | category | flops | bytes accessed | tf_op | source)
XLA Modules:
  0.0 104.5 jit_solution(15764756894311047526)
XLA Ops:
  6.5 0.0 copy-start
  6.5 0.0 reduce-scatter.2.cloned.1.call-start
  6.5 1.2 %fusion.34 = (f32[16,16,256]{2,1,0:T(8,128)S(1)}, f32[16,16,256]{2,1,0:T(8,128)S(1)}) fusion(f32[80,16,256]{2,1,0:T(8,128)} %param.6), kind=kLoop, calls=%fused_computation.64 | loop fusion | bytes 1048576 | tf_op jit(solution)/shard_map/slice | solution.py:18
  7.7 4.9 %collective-permute-start = (f32[16,16,256]{2,1,0:T(8,128)S(1)}, f32[16,16,256]{2,1,0:T(8,128)S(1)}, u32[]{:S(2)}, u32[]{:S(2)}) collective-permute-start(f32[16,16,256]{2,1,0:T(8,128)S(1)} %get-tuple-element.7), channel_id=1, source_target_pairs={{0,2},{1,3},{4,6},{5,7},{8,10},{9,11},{12,14},{13,15},{16,18},{17,... | collective-permute-start | bytes 786440 | tf_op jit(solution)/shard_map/ppermute | solution.py:21
  12.6 1.3 %collective-permute-start.1 = (f32[16,16,256]{2,1,0:T(8,128)S(1)}, f32[16,16,256]{2,1,0:T(8,128)S(1)}, u32[]{:S(2)}, u32[]{:S(2)}) collective-permute-start(f32[16,16,256]{2,1,0:T(8,128)S(1)} %get-tuple-element.8), channel_id=1, source_target_pairs={{2,0},{3,1},{6,4},{7,5},{10,8},{11,9},{14,12},{15,13},{18,16},{19,... | collective-permute-start | bytes 786440 | tf_op jit(solution)/shard_map/ppermute | solution.py:23
  13.9 0.1 reshape.208
  14.0 0.7 iota_compare_fusion.1
  14.7 0.7 add_subtract_fusion
  15.3 0.7 select_reduce_fusion.1
  16.1 0.8 select_reduce_fusion
  16.9 0.1 subtract_multiply_fusion
  16.9 0.5 fusion.10
  17.5 0.6 collective-permute-done
  18.1 4.1 %collective-permute-done.1 = f32[16,16,256]{2,1,0:T(8,128)S(1)} collective-permute-done((f32[16,16,256]{2,1,0:T(8,128)S(1)}, f32[16,16,256]{2,1,0:T(8,128)S(1)}, u32[]{:S(2)}, u32[]{:S(2)}) %collective-permute-start.1) | collective-permute-done | bytes 262176 | tf_op jit(solution)/shard_map/ppermute | solution.py:23
  22.2 0.0 copy-done
  22.2 0.1 pad_maximum_fusion.1
  22.4 1.4 %copy.12 = f32[14,8,16,256]{3,1,2,0:T(8,128)S(1)} copy(f32[14,8,16,256]{3,2,1,0:T(8,128)S(1)} %bitcast.20) | data formatting | bytes 3670016
  23.8 3.2 %fusion.36 = f32[128,4096]{1,0:T(8,128)} fusion(f32[128,112]{1,0:T(8,128)S(1)} %fusion.10, f32[112,4096]{1,0:T(8,128)S(1)} %bitcast.21), kind=kOutput, calls=%fused_computation.66 | convolution fusion | flops 704643072 | bytes 3989504 | tf_op jit(solution)/shard_map/dot_general | solution.py:66
  26.9 0.0 reduce-scatter.2.cloned.1.call-update
  27.0 32.3 %reduce-scatter.2.cloned.1.call-done = f32[64,4096]{1,0:T(8,128)} async-done(((f32[128,4096]{1,0:T(8,128)}), f32[64,4096]{1,0:T(8,128)}) %reduce-scatter.2.cloned.1.call-update) | async-done | bytes 1048592 | tf_op jit(solution)/shard_map/reduce_scatter | solution.py:69
  59.3 0.0 copy-start.2
  59.3 0.0 copy-start.1
  59.3 2.5 %copy.13 = f32[8,8,16,256]{3,2,1,0:T(8,128)} copy(f32[8,8,16,256]{3,1,2,0:T(8,128)} %bitcast.23) | data formatting | bytes 2097152
  61.8 4.6 %all-to-all-start = ((f32[64,16,256]{2,1,0:T(8,128)}), f32[64,16,256]{2,1,0:T(8,128)S(1)}, u32[]{:S(2)}, u32[]{:S(2)}) async-start(f32[64,16,256]{2,1,0:T(8,128)} %bitcast.12), calls=%async_computation.1 | async-start | bytes 2097152 | tf_op jit(solution)/shard_map/all_to_all | solution.py:71
  66.4 0.0 copy-done.2
  66.4 0.6 dynamic-slice
  67.6 0.0 copy-done.1
  67.6 0.2 dynamic-update-slice
  67.8 21.8 %all-reduce.1 = f32[64]{0:T(128)S(1)} all-reduce(f32[64]{0:T(128)S(1)} %dynamic-update-slice), channel_id=1, replica_groups=mesh['blocks'=2,'space'=4,'tm'=2,'span'=2] {'space'}, use_global_device_ids=true, to_apply=%add.1 | all-reduce | flops 64 | bytes 512
  89.6 2.7 %all-to-all-done = f32[64,16,256]{2,1,0:T(8,128)S(1)} async-done(((f32[64,16,256]{2,1,0:T(8,128)}), f32[64,16,256]{2,1,0:T(8,128)S(1)}, u32[]{:S(2)}, u32[]{:S(2)}) %all-to-all-start) | async-done | bytes 1048608 | tf_op jit(solution)/shard_map/all_to_all | solution.py:71
  92.3 0.1 copy.10
  92.4 0.2 fusion.35
  92.6 0.1 collective-permute-start.2
  92.7 0.5 collective-permute-start.3
  93.2 1.4 %collective-permute-done.2 = f32[16,64,1]{2,1,0:T(8,128)S(1)} collective-permute-done((f32[16,64,1]{2,1,0:T(8,128)S(1)}, f32[16,64,1]{2,1,0:T(8,128)S(1)}, u32[]{:S(2)}, u32[]{:S(2)}) %collective-permute-start.2) | collective-permute-done | bytes 4128 | tf_op jit(solution)/shard_map/ppermute | solution.py:23
  94.6 0.7 collective-permute-done.3
  95.4 0.8 fusion.2
  96.2 1.5 %pad_maximum_fusion = f32[16,2,64,256]{3,2,1,0:T(8,128)} fusion(f32[16,1,64,256]{3,2,1,0:T(8,128)S(1)} %get-tuple-element.10, f32[16,1,64,256]{3,2,1,0:T(8,128)S(1)} %get-tuple-element.9), kind=kLoop, calls=%fused_computation | loop fusion | flops 524288 | bytes 4194304 | tf_op jit(solution)/shard_map/stack | solution.py:77
  (6 shorter events, 0.1 us)
Async XLA Ops:
  6.5 15.7 %copy-start = (f32[80,16,256]{2,1,0:T(8,128)S(1)}, f32[80,16,256]{2,1,0:T(8,128)}, u32[]{:S(2)}) copy-start(f32[80,16,256]{2,1,0:T(8,128)} %param.6) | copy-start | bytes 3932164
  6.5 52.7 %reduce-scatter.2.cloned.1.call-start = ((), (), s32[]{:S(2)}) async-start(), calls=%async_computation.2 | async-start | bytes 3145728 | tf_op jit(solution)/shard_map/reduce_scatter | solution.py:69
  7.7 10.4 %collective-permute-start = (f32[16,16,256]{2,1,0:T(8,128)S(1)}, f32[16,16,256]{2,1,0:T(8,128)S(1)}, u32[]{:S(2)}, u32[]{:S(2)}) collective-permute-start(f32[16,16,256]{2,1,0:T(8,128)S(1)} %get-tuple-element.7), channel_id=1, source_target_pairs={{0,2},{1,3},{4,6},{5,7},{8,10},{9,11},{12,14},{13,15},{16,18},{17,... | collective-permute-start | bytes 786440 | tf_op jit(solution)/shard_map/ppermute | solution.py:21
  12.6 9.7 %collective-permute-start.1 = (f32[16,16,256]{2,1,0:T(8,128)S(1)}, f32[16,16,256]{2,1,0:T(8,128)S(1)}, u32[]{:S(2)}, u32[]{:S(2)}) collective-permute-start(f32[16,16,256]{2,1,0:T(8,128)S(1)} %get-tuple-element.8), channel_id=1, source_target_pairs={{2,0},{3,1},{6,4},{7,5},{10,8},{11,9},{14,12},{15,13},{18,16},{19,... | collective-permute-start | bytes 786440 | tf_op jit(solution)/shard_map/ppermute | solution.py:23
  59.3 7.1 %copy-start.2 = (u32[32]{0:T(128)S(1)}, u32[32]{0:T(128)}, u32[]{:S(2)}) copy-start(u32[32]{0:T(128)} %constant.95) | copy-start | bytes 388
  59.3 8.3 %copy-start.1 = (f32[16]{0:T(128)S(1)}, f32[16]{0:T(128)}, u32[]{:S(2)}) copy-start(f32[16]{0:T(128)} %param.11) | copy-start | bytes 196
  61.8 30.5 %all-to-all-start = ((f32[64,16,256]{2,1,0:T(8,128)}), f32[64,16,256]{2,1,0:T(8,128)S(1)}, u32[]{:S(2)}, u32[]{:S(2)}) async-start(f32[64,16,256]{2,1,0:T(8,128)} %bitcast.12), calls=%async_computation.1 | async-start | bytes 2097152 | tf_op jit(solution)/shard_map/all_to_all | solution.py:71
  92.6 2.0 %collective-permute-start.2 = (f32[16,64,1]{2,1,0:T(8,128)S(1)}, f32[16,64,1]{2,1,0:T(8,128)S(1)}, u32[]{:S(2)}, u32[]{:S(2)}) collective-permute-start(f32[16,64,1]{2,1,0:T(8,128)S(1)} %get-tuple-element.11), channel_id=1, source_target_pairs={{1,0},{0,1},{3,2},{2,3},{5,4},{4,5},{7,6},{6,7},{9,8},{8,9},{11,10... | collective-permute-start | bytes 12296 | tf_op jit(solution)/shard_map/ppermute | solution.py:23
  92.7 2.6 %collective-permute-start.3 = (f32[16,64,1]{2,1,0:T(8,128)S(1)}, f32[16,64,1]{2,1,0:T(8,128)S(1)}, u32[]{:S(2)}, u32[]{:S(2)}) collective-permute-start(f32[16,64,1]{2,1,0:T(8,128)S(1)} %get-tuple-element.12), channel_id=1, source_target_pairs={{0,1},{1,0},{2,3},{3,2},{4,5},{5,4},{6,7},{7,6},{8,9},{9,8},{10,11... | collective-permute-start | bytes 12296 | tf_op jit(solution)/shard_map/ppermute | solution.py:21
Sparse Core Ops, SparseCore 0:
  27.1 32.1 reduce-scatter.1
where the time goes:
time: 105 us
  waiting for transfers between devices  42 us (40%)
  blocking collectives  21.8 us (21%)
  between operations  14.1 us (13%)
  starting transfers between devices  11.3 us (11%)
  local copies, waits for them, and re-layouts  6.28 us (6%)
  other arithmetic  5.39 us (5%)
  matrix products  3.72 us (4%)
    reduce_scatter x1, waiting for transfers between devices, shards(): summed = lax.psum_scatter(partial, 'tm', scatter_dimension=0, tiled=True)  32.3 us
    unnamed x1, blocking collectives  21.8 us
    ppermute x2, waiting for transfers between devices, extended(): lax.ppermute(head, axis, [((i + 1) % count, i) for i in range(ends)])  5.52 us
    ppermute x2, starting transfers between devices, extended(): lax.ppermute(tail, axis, [(i, (i + 1) % count) for i in range(ends)])  5.36 us
    unnamed x11, local copies, waits for them, and re-layouts  4.74 us
    all_to_all x1, starting transfers between devices, shards(): lax.all_to_all(summed, 'space', split_axis=0, concat_axis=1, tiled=True)  4.59 us
    dot_general x1, matrix products, shards(): jnp.dot(combined, reach.reshape(reach_len, rows_dev * span_cells), precis...  3.18 us
    all_to_all x1, waiting for transfers between devices, shards(): lax.all_to_all(summed, 'space', split_axis=0, concat_axis=1, tiled=True)  2.73 us
  transfers between devices with their start and end apart: 6, of which 6 were waited for; matrix products, arithmetic and copies ran while one was open for 4% of the time, Pallas kernels for 0%

commit v1 on v0

--- a/solution.py
+++ b/solution.py
@@ -8,6 +8,28 @@
 NT = 256
 BW = 8
 NL = 8
+
+
+def in_blocks(x, dim, peers):
+    before, after = (x.shape[:dim], x.shape[dim + 1 :])
+    return jnp.moveaxis(x.reshape(*before, peers, -1, *after), dim, 0)
+
+
+def in_order(parts, dim):
+    shape = list(parts.shape[1:])
+    shape[dim] *= parts.shape[0]
+    return jnp.moveaxis(parts, 0, dim).reshape(shape)
+
+
+def rotated_exchange(x, axis, split_dim, concat_dim):
+    peers, place = (lax.axis_size(axis), lax.axis_index(axis))
+    parts = in_blocks(x, split_dim, peers)
+    finished = [parts[place]]
+    for step in range(1, peers):
+        sent = parts[(place + step) % peers]
+        finished.append(lax.ppermute(sent, axis, [(i, (i + step) % peers) for i in range(peers)]))
+    parts = jnp.stack(finished)[(place - jnp.arange(peers)) % peers]
+    return in_order(parts, concat_dim)
 
 
 def extended(cells, sides, width, closed):
@@ -68,7 +90,7 @@
     )
     summed = lax.psum_scatter(partial, "tm", scatter_dimension=0, tiled=True)
     summed = summed.reshape(n_space * own, rows_dev, span_cells)
-    fields = lax.all_to_all(summed, "space", split_axis=0, concat_axis=1, tiled=True)
+    fields = rotated_exchange(summed, "space", 0, 1)
     metric = lax.all_gather(row_metric, "space", tiled=True)
     row_padded = jnp.pad(fields, ((0, 0), (1, 1), (0, 0)))
     along_rows = 0.5 * metric[None, :, None] * (row_padded[:, 2:, :] - row_padded[:, :-2, :])

time: 105 us -> 101 us (0.962)
  waiting for transfers between devices: 42 us -> 39.2 us
  blocking collectives: 21.8 us -> 20.4 us
    all_to_all x1 -> x0, starting transfers between devices: 4.59 us -> none  [shards(): lax.all_to_all(summed, 'space', split_axis=0, concat_axis=1, tiled=True)]
    ppermute x0 -> x3, starting transfers between devices: none -> 4.47 us  [rotated_exchange(): lax.ppermute(sent, axis, [(i, (i + step) % peers) for i in range(peers)])]
    all_to_all x1 -> x0, waiting for transfers between devices: 2.73 us -> none  [shards(): lax.all_to_all(summed, 'space', split_axis=0, concat_axis=1, tiled=True)]
    unnamed x1, blocking collectives: 21.8 us -> 20.4 us
  transfers between devices with their start and end apart: 6 -> 8, of which waited for: 6 -> 5; matrix products, arithmetic and copies ran while one was open for 4% -> 4% of each run, Pallas kernels for 0% -> 0%
where the time goes in v1:
time: 101 us; the launch traced here: 100 us
  waiting for transfers between devices  39.2 us (39%)
  blocking collectives  20.4 us (20%)
  between operations  14.3 us (14%)
  starting transfers between devices  11.2 us (11%)
  local copies, waits for them, and re-layouts  6.03 us (6%)
  other arithmetic  5.48 us (5%)
  matrix products  3.72 us (4%)
    reduce_scatter x1, waiting for transfers between devices, shards(): summed = lax.psum_scatter(partial, 'tm', scatter_dimension=0, tiled=True)  32.3 us
    unnamed x1, blocking collectives  20.4 us
    ppermute x2, waiting for transfers between devices, extended(): lax.ppermute(head, axis, [((i + 1) % count, i) for i in range(ends)])  5.52 us
    ppermute x2, starting transfers between devices, extended(): lax.ppermute(tail, axis, [(i, (i + 1) % count) for i in range(ends)])  5.36 us
    ppermute x3, starting transfers between devices, rotated_exchange(): lax.ppermute(sent, axis, [(i, (i + step) % peers) for i in range(peers)])  4.47 us
    unnamed x11, local copies, waits for them, and re-layouts  3.77 us
    dot_general x1, matrix products, shards(): jnp.dot(combined, reach.reshape(reach_len, rows_dev * span_cells), precis...  3.18 us
    another operation x2, other arithmetic, shards(): return jnp.stack((along_rows, along_span), axis=1)  2.32 us
  transfers between devices with their start and end apart: 8, of which 5 were waited for; matrix products, arithmetic and copies ran while one was open for 4% of the time, Pallas kernels for 0%

profile of v1, /device:TPU:0, one launch (start us, length us, event | category | flops | bytes accessed | tf_op | source)
XLA Modules:
  0.0 100.3 jit_solution(2345763963756720093)
XLA Ops:
  6.5 0.0 copy-start
  6.5 0.0 reduce-scatter.2.cloned.1.call-start
  6.5 1.2 %fusion.36 = (f32[16,16,256]{2,1,0:T(8,128)S(1)}, f32[16,16,256]{2,1,0:T(8,128)S(1)}) fusion(f32[80,16,256]{2,1,0:T(8,128)} %param.6), kind=kLoop, calls=%fused_computation.77 | loop fusion | bytes 1048576 | tf_op jit(solution)/shard_map/slice | solution.py:40
  7.7 4.9 %collective-permute-start = (f32[16,16,256]{2,1,0:T(8,128)S(1)}, f32[16,16,256]{2,1,0:T(8,128)S(1)}, u32[]{:S(2)}, u32[]{:S(2)}) collective-permute-start(f32[16,16,256]{2,1,0:T(8,128)S(1)} %get-tuple-element.7), channel_id=1, source_target_pairs={{0,2},{1,3},{4,6},{5,7},{8,10},{9,11},{12,14},{13,15},{16,18},{17,... | collective-permute-start | bytes 786440 | tf_op jit(solution)/shard_map/ppermute | solution.py:43
  12.6 1.3 %collective-permute-start.1 = (f32[16,16,256]{2,1,0:T(8,128)S(1)}, f32[16,16,256]{2,1,0:T(8,128)S(1)}, u32[]{:S(2)}, u32[]{:S(2)}) collective-permute-start(f32[16,16,256]{2,1,0:T(8,128)S(1)} %get-tuple-element.8), channel_id=1, source_target_pairs={{2,0},{3,1},{6,4},{7,5},{10,8},{11,9},{14,12},{15,13},{18,16},{19,... | collective-permute-start | bytes 786440 | tf_op jit(solution)/shard_map/ppermute | solution.py:45
  13.9 0.1 reshape.257
  14.0 0.7 iota_compare_fusion.1
  14.7 0.7 add_subtract_fusion
  15.3 0.7 select_reduce_fusion.1
  16.1 0.8 select_reduce_fusion
  16.9 0.1 subtract_multiply_fusion
  16.9 0.5 fusion.10
  17.5 0.6 collective-permute-done
  18.1 4.1 %collective-permute-done.1 = f32[16,16,256]{2,1,0:T(8,128)S(1)} collective-permute-done((f32[16,16,256]{2,1,0:T(8,128)S(1)}, f32[16,16,256]{2,1,0:T(8,128)S(1)}, u32[]{:S(2)}, u32[]{:S(2)}) %collective-permute-start.1) | collective-permute-done | bytes 262176 | tf_op jit(solution)/shard_map/ppermute | solution.py:45
  22.2 0.0 copy-done
  22.2 0.1 pad_maximum_fusion.1
  22.4 1.4 %copy.12 = f32[14,8,16,256]{3,1,2,0:T(8,128)S(1)} copy(f32[14,8,16,256]{3,2,1,0:T(8,128)S(1)} %bitcast.30) | data formatting | bytes 3670016
  23.8 3.2 %fusion.38 = f32[128,4096]{1,0:T(8,128)} fusion(f32[128,112]{1,0:T(8,128)S(1)} %fusion.10, f32[112,4096]{1,0:T(8,128)S(1)} %bitcast.31), kind=kOutput, calls=%fused_computation.79 | convolution fusion | flops 704643072 | bytes 3989504 | tf_op jit(solution)/shard_map/dot_general | solution.py:88
  26.9 0.0 reduce-scatter.2.cloned.1.call-update
  27.0 32.3 %reduce-scatter.2.cloned.1.call-done = f32[64,4096]{1,0:T(8,128)} async-done(((f32[128,4096]{1,0:T(8,128)}), f32[64,4096]{1,0:T(8,128)}) %reduce-scatter.2.cloned.1.call-update) | async-done | bytes 1048592 | tf_op jit(solution)/shard_map/reduce_scatter | solution.py:91
  59.3 0.0 copy-start.2
  59.3 0.0 copy-start.1
  59.3 1.6 %copy.13 = f32[8,8,16,256]{3,2,1,0:T(8,128)S(1)} copy(f32[8,8,16,256]{3,1,2,0:T(8,128)} %bitcast.34) | data formatting | bytes 2097152
  60.9 0.1 constant_dynamic-slice_fusion
  61.0 3.4 %collective-permute-start.4 = (f32[16,16,256]{2,1,0:T(8,128)S(1)}, f32[16,16,256]{2,1,0:T(8,128)S(1)}, u32[]{:S(2)}, u32[]{:S(2)}) collective-permute-start(f32[16,16,256]{2,1,0:T(8,128)S(1)} %get-tuple-element.14), channel_id=1, source_target_pairs={{0,12},{4,0},{8,4},{12,8},{1,13},{5,1},{9,5},{13,9},{2,14},{6,2},{... | collective-permute-start | bytes 786440 | tf_op jit(solution)/shard_map/ppermute | solution.py:30
  64.3 0.0 collective-permute-start.3
  64.3 1.1 %collective-permute-start.2 = (f32[16,16,256]{2,1,0:T(8,128)S(1)}, f32[16,16,256]{2,1,0:T(8,128)S(1)}, u32[]{:S(2)}, u32[]{:S(2)}) collective-permute-start(f32[16,16,256]{2,1,0:T(8,128)S(1)} %get-tuple-element.16), channel_id=1, source_target_pairs={{0,4},{4,8},{8,12},{12,0},{1,5},{5,9},{9,13},{13,1},{2,6},{6,10},{... | collective-permute-start | bytes 786440 | tf_op jit(solution)/shard_map/ppermute | solution.py:30
  65.4 0.0 copy-done.2
  65.4 0.6 dynamic-slice
  66.7 0.0 copy-done.1
  66.7 0.2 dynamic-update-slice
  66.9 20.4 %all-reduce.1 = f32[64]{0:T(128)S(1)} all-reduce(f32[64]{0:T(128)S(1)} %dynamic-update-slice), channel_id=1, replica_groups=mesh['blocks'=2,'space'=4,'tm'=2,'span'=2] {'space'}, use_global_device_ids=true, to_apply=%add.1 | all-reduce | flops 64 | bytes 512
  87.4 0.0 collective-permute-done.4
  87.4 0.0 collective-permute-done.3
  87.4 0.0 collective-permute-done.2
  87.4 0.1 pad_maximum_fusion.4
  87.5 0.6 gather_fusion
  88.1 0.1 copy.10
  88.2 0.2 fusion.37
  88.4 0.1 collective-permute-start.5
  88.5 0.5 collective-permute-start.6
  89.0 1.4 %collective-permute-done.5 = f32[16,64,1]{2,1,0:T(8,128)S(1)} collective-permute-done((f32[16,64,1]{2,1,0:T(8,128)S(1)}, f32[16,64,1]{2,1,0:T(8,128)S(1)}, u32[]{:S(2)}, u32[]{:S(2)}) %collective-permute-start.5) | collective-permute-done | bytes 4128 | tf_op jit(solution)/shard_map/ppermute | solution.py:45
  90.4 0.7 collective-permute-done.6
  91.1 0.8 fusion.2
  92.0 1.5 %pad_maximum_fusion = f32[16,2,64,256]{3,2,1,0:T(8,128)} fusion(f32[16,1,64,256]{3,2,1,0:T(8,128)S(1)} %get-tuple-element.10, f32[16,1,64,256]{3,2,1,0:T(8,128)S(1)} %get-tuple-element.9), kind=kLoop, calls=%fused_computation.1 | loop fusion | flops 524288 | bytes 4194304 | tf_op jit(solution)/shard_map/stack | solution.py:99
  (8 shorter events, 0.1 us)
Async XLA Ops:
  6.5 15.7 %copy-start = (f32[80,16,256]{2,1,0:T(8,128)S(1)}, f32[80,16,256]{2,1,0:T(8,128)}, u32[]{:S(2)}) copy-start(f32[80,16,256]{2,1,0:T(8,128)} %param.6) | copy-start | bytes 3932164
  6.5 52.7 %reduce-scatter.2.cloned.1.call-start = ((), (), s32[]{:S(2)}) async-start(), calls=%async_computation.1 | async-start | bytes 3145728 | tf_op jit(solution)/shard_map/reduce_scatter | solution.py:91
  7.7 10.4 %collective-permute-start = (f32[16,16,256]{2,1,0:T(8,128)S(1)}, f32[16,16,256]{2,1,0:T(8,128)S(1)}, u32[]{:S(2)}, u32[]{:S(2)}) collective-permute-start(f32[16,16,256]{2,1,0:T(8,128)S(1)} %get-tuple-element.7), channel_id=1, source_target_pairs={{0,2},{1,3},{4,6},{5,7},{8,10},{9,11},{12,14},{13,15},{16,18},{17,... | collective-permute-start | bytes 786440 | tf_op jit(solution)/shard_map/ppermute | solution.py:43
  12.6 9.7 %collective-permute-start.1 = (f32[16,16,256]{2,1,0:T(8,128)S(1)}, f32[16,16,256]{2,1,0:T(8,128)S(1)}, u32[]{:S(2)}, u32[]{:S(2)}) collective-permute-start(f32[16,16,256]{2,1,0:T(8,128)S(1)} %get-tuple-element.8), channel_id=1, source_target_pairs={{2,0},{3,1},{6,4},{7,5},{10,8},{11,9},{14,12},{15,13},{18,16},{19,... | collective-permute-start | bytes 786440 | tf_op jit(solution)/shard_map/ppermute | solution.py:45
  59.3 6.2 %copy-start.2 = (u32[32]{0:T(128)S(1)}, u32[32]{0:T(128)}, u32[]{:S(2)}) copy-start(u32[32]{0:T(128)} %constant.131) | copy-start | bytes 388
  59.3 7.4 %copy-start.1 = (f32[16]{0:T(128)S(1)}, f32[16]{0:T(128)}, u32[]{:S(2)}) copy-start(f32[16]{0:T(128)} %param.11) | copy-start | bytes 196
  61.0 26.4 %collective-permute-start.4 = (f32[16,16,256]{2,1,0:T(8,128)S(1)}, f32[16,16,256]{2,1,0:T(8,128)S(1)}, u32[]{:S(2)}, u32[]{:S(2)}) collective-permute-start(f32[16,16,256]{2,1,0:T(8,128)S(1)} %get-tuple-element.14), channel_id=1, source_target_pairs={{0,12},{4,0},{8,4},{12,8},{1,13},{5,1},{9,5},{13,9},{2,14},{6,2},{... | collective-permute-start | bytes 786440 | tf_op jit(solution)/shard_map/ppermute | solution.py:30
  64.3 23.1 %collective-permute-start.3 = (f32[16,16,256]{2,1,0:T(8,128)S(1)}, f32[16,16,256]{2,1,0:T(8,128)S(1)}, u32[]{:S(2)}, u32[]{:S(2)}) collective-permute-start(f32[16,16,256]{2,1,0:T(8,128)S(1)} %get-tuple-element.15), channel_id=1, source_target_pairs={{0,8},{4,12},{8,0},{12,4},{1,9},{5,13},{9,1},{13,5},{2,10},{6,14},... | collective-permute-start | bytes 786440 | tf_op jit(solution)/shard_map/ppermute | solution.py:30
  64.3 23.1 %collective-permute-start.2 = (f32[16,16,256]{2,1,0:T(8,128)S(1)}, f32[16,16,256]{2,1,0:T(8,128)S(1)}, u32[]{:S(2)}, u32[]{:S(2)}) collective-permute-start(f32[16,16,256]{2,1,0:T(8,128)S(1)} %get-tuple-element.16), channel_id=1, source_target_pairs={{0,4},{4,8},{8,12},{12,0},{1,5},{5,9},{9,13},{13,1},{2,6},{6,10},{... | collective-permute-start | bytes 786440 | tf_op jit(solution)/shard_map/ppermute | solution.py:30
  88.4 2.0 %collective-permute-start.5 = (f32[16,64,1]{2,1,0:T(8,128)S(1)}, f32[16,64,1]{2,1,0:T(8,128)S(1)}, u32[]{:S(2)}, u32[]{:S(2)}) collective-permute-start(f32[16,64,1]{2,1,0:T(8,128)S(1)} %get-tuple-element.11), channel_id=1, source_target_pairs={{1,0},{0,1},{3,2},{2,3},{5,4},{4,5},{7,6},{6,7},{9,8},{8,9},{11,10... | collective-permute-start | bytes 12296 | tf_op jit(solution)/shard_map/ppermute | solution.py:45
  88.5 2.6 %collective-permute-start.6 = (f32[16,64,1]{2,1,0:T(8,128)S(1)}, f32[16,64,1]{2,1,0:T(8,128)S(1)}, u32[]{:S(2)}, u32[]{:S(2)}) collective-permute-start(f32[16,64,1]{2,1,0:T(8,128)S(1)} %get-tuple-element.12), channel_id=1, source_target_pairs={{0,1},{1,0},{2,3},{3,2},{4,5},{5,4},{6,7},{7,6},{8,9},{9,8},{10,11... | collective-permute-start | bytes 12296 | tf_op jit(solution)/shard_map/ppermute | solution.py:43
Sparse Core Ops, SparseCore 0:
  27.1 32.1 reduce-scatter.1
